TPU v7x, 128 devices: a whole 4x4x4 slice. The times are simulated.
128 devices in a mesh: tm: 8 (over x, z_hi), tile: 16 (over y, z_lo, core).
Axes of the slice: x: 4, y: 4, z: 4 (z_hi: 2, z_lo: 2; z = z_hi * 2 + z_lo), core: 2. Of those that a mesh axis runs over, the one named last changes fastest.
Arguments:
- frames: bfloat16 [32, 64, 128, 256], P('tm', 'tile'), may hold values from -20 to 20
- first_gain: float32 [256], replicated, may hold values from 0.1 to 1.9
- first_bias: float32 [256], replicated, may hold values from -3 to 3
- first_weight: bfloat16 [3, 3, 3, 256, 256], replicated, may hold values from -0.078125 to 0.078125
- second_gain: float32 [256], replicated, may hold values from 0.1 to 1.9
- second_bias: float32 [256], replicated, may hold values from -3 to 3
- second_weight: bfloat16 [3, 3, 3, 256, 256], replicated, may hold values from -0.1875 to 0.1875
- latent_weight: bfloat16 [256, 16], replicated, may hold values from -0.375 to 0.375
Outputs:
- features: bfloat16 [32, 64, 128, 256], P('tm', 'tile')
- tokens: bfloat16 [32, 32, 4096], P('tm', None, 'tile')
All inputs are finite; a program needn't handle non-finite values.
Results may differ from a plain program's by a relative error of at most 0.012.
Values may be sent and summed in bfloat16 or wider, within the bound.
A program may use at most 128 MiB of HBM per device.

v0:
```python
import functools

import jax
import jax.numpy as jnp
from jax import lax
from jax.experimental import pallas as pl
from jax.experimental.pallas import tpu as pltpu
from jax.sharding import PartitionSpec as P

GROUPS = 32
MESH = pl.DeviceIdType.MESH
F32, BF16 = jnp.float32, jnp.bfloat16
COLS, STEP, RUNS = 128, 16, 8


def iota(shape, dim):
    return lax.broadcasted_iota(jnp.int32, shape, dim)


def mm(a, b):
    return jnp.dot(a, b, preferred_element_type=F32)


def kernel(
    x, params, w1, w2, feat, tok,
    raw, final, first, second, act, mixed, acc, taps1, taps2, blend1, blend2, rows, spread, back, latent, groups, outbox, inbox,
    part1, part2, part3, part4, load_sem, out_sem, hs1, hr1, hs2, hr2, as1, ar1, as2, ar2, as3, ar3, as4, ar4, ts, tr,
):
    tm, tile = lax.axis_index("tm"), lax.axis_index("tile")
    times, tiles = 8, 16
    core = lax.rem(tile, 2)
    cx, cy, cz = tm // 2, tile // 4, lax.rem(tm, 2) * 2 + lax.rem(tile // 2, 2)

    def dev(t, h):
        return {"tm": t, "tile": h}

    def at_chip(i, j, k, c):
        return dev(i * 2 + k // 2, j * 4 + lax.rem(k, 2) * 2 + c)

    def send(src, dst, s, r, device):
        return pltpu.make_async_remote_copy(
            src_ref=src, dst_ref=dst, send_sem=s, recv_sem=r, device_id=device, device_id_type=MESH
        )

    tile_peers = [dev(tm, lax.rem(tile + k, tiles)) for k in range(1, tiles)]
    near_peers = [
        at_chip(cx, cy, lax.rem(cz + k // 2, 4), lax.rem(core + k % 2, 2)) for k in (4, 5, 2, 3, 6, 7, 1)
    ]
    far_peers = [
        at_chip(lax.rem(cx + k // 4, 4), lax.rem(cy + k % 4, 4), cz, core) for k in (10, 9, 11, 6, 14, 2, 8, 5, 7, 13, 15, 1, 3, 4, 12)
    ]
    sides = [
        dev(lax.rem(tm + i, times), lax.rem(tile + j, tiles)) for i in (1, times - 1) for j in (0, 1, tiles - 1)
    ]
    peers = tile_peers + near_peers + far_peers + sides

    loads = [pltpu.make_async_copy(x.at[f], raw.at[f], load_sem.at[f]) for f in range(4)]
    load_w1 = pltpu.make_async_copy(w1, taps1, load_sem.at[4])
    load_w2 = pltpu.make_async_copy(w2, taps2, load_sem.at[5])
    barrier = pltpu.get_barrier_semaphore()
    for f in range(4):
        loads[f].start()
    for peer in peers:
        pl.semaphore_signal(barrier, inc=1, device_id=peer, device_id_type=MESH)
    load_w1.start()

    zero = jnp.zeros((8, 256), F32)
    sums = (zero, zero)
    for f in range(4):
        loads[f].wait()

        def add_row(r, sums, f=f):
            v = raw[f, r].astype(F32).reshape(COLS // 8, 8, 256)
            return sums[0] + v.sum(axis=0), sums[1] + (v * v).sum(axis=0)

        sums = lax.fori_loop(0, 4, add_row, sums, unroll=True)

    class Totals:
        def __init__(self, wide_part, narrow_part, s1, r1, s2, r2):
            self.parts = (wide_part, narrow_part)
            self.copies = [
                [
                    send(part.at[pl.ds(0, 1)], part.at[pl.ds(k + 1, 1)], s.at[k], r.at[k], peer)
                    for k, peer in enumerate(group)
                ]
                for part, s, r, group in ((wide_part, s1, r1, near_peers), (narrow_part, s2, r2, far_peers))
            ]

        def begin(self, sums):
            own = [jnp.sum(s, axis=0, keepdims=True) for s in sums]
            self.parts[0][0:1] = jnp.concatenate(own, axis=1)
            for copy in self.copies[0]:
                copy.start()

        def middle(self):
            for copy in self.copies[0]:
                copy.wait_recv()
            self.parts[1][0:1] = jnp.sum(self.parts[0][...], axis=0, keepdims=True)
            for copy in self.copies[1]:
                copy.start()

        def end(self):
            for copy in self.copies[1]:
                copy.wait_recv()
            return jnp.sum(self.parts[1][...], axis=0, keepdims=True)

        def sent(self):
            for copy in self.copies[0] + self.copies[1]:
                copy.wait_send()

    totals1 = Totals(part1, part2, as1, ar1, as2, ar2)
    totals2 = Totals(part3, part4, as3, ar3, as4, ar4)

    class Halo:
        def __init__(self, buf, ss, rs):
            def copy(k, src, dst, device):
                return send(src, dst, ss.at[k], rs.at[k], device)

            right, left, later = dev(tm, tile + 1), dev(tm, tile - 1), dev(tm + 1, tile)
            more, some = tm < times - 1, tm > 0
            self.rows, self.edge, self.rest, self.forward = {}, {}, {}, {}
            for k, f in ((0, 4), (1, 2)):
                pair = pl.ds(f, 2)
                self.rows[f] = [
                    (copy(2 * k, buf.at[pair, 4], buf.at[pair, 0], right), tile < tiles - 1, tile > 0),
                    (copy(2 * k + 1, buf.at[pair, 1], buf.at[pair, 5], left), tile > 0, tile < tiles - 1),
                ]
            late, past = pl.ds(4, 2), pl.ds(0, 2)
            edge, rest = 4 - 3 * core, pl.ds(1 + core, 3)
            self.edge = [(copy(4, buf.at[late, edge], buf.at[past, edge], later), more, some)]
            for f in (1, 0):
                self.rest[f] = [(copy(5 + f, buf.at[4 + f, rest], buf.at[f, rest], later), more, some)]
            self.diagonal = [
                (
                    copy(7, buf.at[late, 4], buf.at[past, 0], dev(tm + 1, tile + 1)),
                    more & (core == 1) & (tile < tiles - 1),
                    some & (core == 0) & (tile > 0),
                ),
                (
                    copy(8, buf.at[late, 1], buf.at[past, 5], dev(tm + 1, tile - 1)),
                    more & (core == 0) & (tile > 0),
                    some & (core == 1) & (tile < tiles - 1),
                ),
            ]
            self.forward = [
                (copy(9, buf.at[past, 4], buf.at[past, 0], right), some & (core == 0), some & (core == 1)),
                (copy(10, buf.at[past, 1], buf.at[past, 5], left), some & (core == 1), some & (core == 0)),
            ]
            self.all = self.rows[4] + self.rows[2] + self.edge + self.rest[1] + self.rest[0]
            self.all = self.all + self.diagonal + self.forward

    def start(copies):
        for copy, sends, _ in copies:
            pl.when(sends)(copy.start)

    def received(copies):
        for copy, _, receives in copies:
            pl.when(receives)(copy.wait_recv)

    def sent(copies):
        for copy, sends, _ in copies:
            pl.when(sends)(copy.wait_send)

    halo1, halo2 = Halo(first, hs1, hr1), Halo(second, hs2, hr2)

    pl.semaphore_wait(barrier, len(peers))
    totals1.begin(sums)

    square = (COLS, COLS)
    a, b = iota(square, 0), iota(square, 1)
    spread[...] = (b == RUNS * (a % STEP) + a // STEP).astype(F32).astype(BF16)
    back[...] = (a == RUNS * (b % STEP) + b // STEP).astype(F32).astype(BF16)

    def place(i, _):
        f, r = i // 4, lax.rem(i, 4)
        first[2 + f, 1 + r] = mm(spread[...], raw[f, r]).astype(BF16)
        return 0

    lax.fori_loop(0, 16, place, 0, unroll=4)
    start(halo1.rows[4] + halo1.rows[2])
    load_w2.start()

    wide = (16, 256)
    repeat = (iota(wide, 0) == iota(wide, 1) % 16).astype(F32).astype(BF16)
    latent[...] = lax.dot_general(
        params[0:16].astype(BF16), repeat, (((0,), (0,)), ((), ())), preferred_element_type=F32
    ).astype(BF16)
    shape = (256, 256)
    groups[...] = (iota(shape, 0) // 8 == iota(shape, 1) // 8).astype(F32).astype(BF16)
    none = jnp.zeros((COLS + 2 * STEP, 256), BF16)
    for outside, r in ((tile == 0, 0), (tile == tiles - 1, 5)):

        @pl.when(outside)
        def _(r=r):
            for f in range(6):
                act[f * 6 + r] = none

    @pl.when(tm == 0)
    def _():
        for k in range(12):
            act[k] = none

    def blend(taps, into):
        def some(k, _):
            b, c = k // 3, lax.rem(k, 3)
            outer = 0.5 * (taps[0, b, c].astype(F32) + taps[2, b, c].astype(F32))
            inner = 0.5 * taps[1, b, c].astype(F32)
            into[0, b, c] = (outer + inner).astype(BF16)
            into[1, b, c] = (outer - inner).astype(BF16)
            return 0

        lax.fori_loop(0, 9, some, 0)

    load_w1.wait()
    blend(taps1, blend1)
    totals1.middle()
    start(halo1.edge + halo1.diagonal + halo1.rest[1] + halo1.rest[0])
    load_w2.wait()
    blend(taps2, blend2)

    members = float(32 * 64 * 128 * 8)

    def scales(total, gain, bias):
        both = jnp.concatenate([total[:, :256], total[:, 256:]], axis=0)
        high = both.astype(BF16).astype(F32)
        middle = (both - high).astype(BF16).astype(F32)
        low = both - high - middle
        split = jnp.concatenate([high, middle, low, jnp.zeros((2, 256), F32)], axis=0).astype(BF16)
        split = mm(split, groups[...])
        both = split[0:2] + split[2:4] + split[4:6]
        average = both[0:1] / members
        variance = both[1:2] / members - average * average
        factor = lax.rsqrt(variance + 1e-06) * gain
        return 0.5 * factor, 0.5 * (bias - average * factor)

    def norm_row(buf, f, r, scale):
        v = buf[f, r].astype(F32) * scale[0] + scale[1]
        y = v + v * jnp.tanh(v)
        at = f * 6 + r
        act[at, STEP : STEP + COLS] = y.astype(BF16)
        edge = iota((STEP, 256), 0)
        before = pltpu.roll(y[COLS - STEP :], 1, axis=0)
        after = pltpu.roll(y[:STEP], STEP - 1, axis=0)
        act[at, 0:STEP] = jnp.where(edge == 0, 0.0, before).astype(BF16)
        act[at, STEP + COLS :] = jnp.where(edge == STEP - 1, 0.0, after).astype(BF16)

    def norm_own(buf, scale):
        def some(i, _):
            norm_row(buf, 2 + i // 4, 1 + lax.rem(i, 4), scale)
            return 0

        lax.fori_loop(0, 16, some, 0, unroll=8)

    def norm_sides(buf, scale):
        for inside, r in ((tile > 0, 0), (tile < tiles - 1, 5)):

            @pl.when(inside)
            def _(r=r):
                for f in range(2, 6):
                    norm_row(buf, f, r, scale)

    def norm_past(buf, f, scale):
        @pl.when(tm > 0)
        def _():
            for r in range(1, 5):
                norm_row(buf, f, r, scale)

        for inside, r in ((tile > 0, 0), (tile < tiles - 1, 5)):

            @pl.when(inside & (tm > 0))
            def _(r=r):
                norm_row(buf, f, r, scale)

    def mix(q):
        def some(r, _):
            d = [act[(2 - 2 * q + i) * 6 + r] for i in range(4)]
            mixed[r] = d[0] - d[2]
            mixed[6 + r] = d[1] + d[2]
            mixed[12 + r] = d[2] - d[1]
            mixed[18 + r] = d[1] - d[3]
            return 0

        lax.fori_loop(0, 6, some, 0, unroll=2)

    def product(taps, j):
        total = None
        for b in range(3):
            at = pl.ds(j * 6 + b, 4)
            piece = jnp.concatenate(
                [mixed[at, STEP * c : STEP * c + COLS, :].reshape(4 * COLS, 256) for c in range(3)], axis=1
            )
            term = mm(piece, taps[b].reshape(768, 256))
            total = term if total is None else total + term
        return total

    def direct(taps, units):
        total = None
        for o, a in units:
            for b in range(3):
                at = pl.ds((o + a) * 6 + b, 4)
                piece = jnp.concatenate(
                    [act[at, STEP * c : STEP * c + COLS, :].reshape(4 * COLS, 256) for c in range(3)], axis=1
                )
                term = mm(piece, taps[a, b].reshape(768, 256))
                total = term if total is None else total + term
        return total

    def conv(taps, blended, halo, buf, scale, done, between, arrived):
        mix(0)
        m1, m2 = product(blended.at[0], 1), product(blended.at[1], 2)
        y0, y1 = m1 + m2, m1 - m2
        acc[0] = y0 + product(taps.at[0], 0)
        acc[1] = y1 - product(taps.at[2], 3)
        carry = done(2, 0, (zero, zero))
        carry = done(2, 1, carry)
        between()
        acc[0] = direct(taps, ((0, 2),))
        acc[1] = direct(taps, ((1, 1), (1, 2)))
        received(halo.diagonal + halo.forward + halo.rest[1])
        norm_past(buf, 1, scale)
        received(halo.rest[0])
        arrived()
        norm_past(buf, 0, scale)
        acc[1] += direct(taps, ((1, 0),))
        acc[0] += direct(taps, ((0, 1), (0, 0)))
        return done(0, 1, done(0, 0, carry))

    scale = scales(totals1.end(), params[16:17], params[17:18])
    norm_own(first, scale)
    received(halo1.rows[4] + halo1.rows[2])
    norm_sides(first, scale)
    received(halo1.edge)
    start(halo1.forward)

    def keep(o, half, sums):
        hidden = acc[half].astype(BF16)
        second[2 + o + half, pl.ds(1, 4)] = hidden.reshape(4, COLS, 256)
        v = hidden.astype(F32).reshape(4 * COLS // 8, 8, 256)
        return sums[0] + v.sum(axis=0), sums[1] + (v * v).sum(axis=0)

    sums = conv(
        taps1, blend1, halo1, first, scale, keep, lambda: None, lambda: start(halo2.rows[4] + halo2.edge + halo2.diagonal)
    )

    totals2.begin(sums)
    start(halo2.rows[2])
    totals2.middle()
    start(halo2.rest[1] + halo2.rest[0])
    scale = scales(totals2.end(), params[18:19], params[19:20])
    norm_own(second, scale)
    received(halo2.rows[4] + halo2.rows[2])
    norm_sides(second, scale)
    received(halo2.edge)
    start(halo2.forward)

    def finish_latents(o, half):
        frames = first[2 + o, pl.ds(1, 4)].reshape(4 * COLS, 256).astype(F32)
        features = (frames + acc[half]).astype(BF16)
        final[o] = features.reshape(4, COLS, 256)
        latents = mm(features, latent[...])
        lane = iota((STEP, 256), 1) // 16
        for i in range(2):
            block = jnp.zeros((STEP, 256), F32)
            for p in range(2):
                for s in range(RUNS):
                    at = (2 * i + p) * COLS + s * STEP
                    here = lane == 4 * (s // 2) + 2 * p + s % 2
                    block = jnp.where(here, latents[at : at + STEP], block)
            rows[pl.ds(pl.multiple_of((2 * o + i) * STEP, STEP), STEP)] = block

    def finish_features(o):
        for r in range(4):
            raw[o, r] = mm(back[...], final[o, r]).astype(BF16)
        pltpu.make_async_copy(raw.at[o], feat.at[o], out_sem.at[o]).start()

    def finish(o, half, carry):
        finish_latents(o + half, half)
        return carry

    def finish_early():
        finish_features(3)
        finish_features(2)

    conv(taps2, blend2, halo2, second, scale, finish, finish_early, lambda: None)

    turn = (b == (a % 8) * 16 + a // 8).astype(F32).astype(BF16)
    outbox[...] = mm(turn, rows[...].astype(BF16)).reshape(16, 8, 256)
    copies = []
    for k in range(1, tiles):
        to = lax.rem(tile + k, tiles)
        copies.append(send(outbox.at[to], inbox.at[tile], ts.at[k], tr.at[k], dev(tm, to)))
    for copy in copies:
        copy.start()

    finish_features(1)
    finish_features(0)
    inbox[tile] = outbox[tile]
    turn = (b == ((a % 32) // 2) * 8 + (a // 32) * 2 + a % 2).astype(F32).astype(BF16)
    for k in range(1, tiles):
        source = lax.rem(tile + tiles - k, tiles)
        send(outbox.at[source], inbox.at[source], ts.at[k], tr.at[k], dev(tm, source)).wait_recv()
    tok[...] = mm(turn, inbox[...].reshape(128, 256).astype(BF16)).astype(BF16).reshape(4, 32, 256)
    for f in range(4):
        pltpu.make_async_copy(raw.at[f], feat.at[f], out_sem.at[f]).wait()
    for copy in copies:
        copy.wait_send()
    totals1.sent()
    totals2.sent()
    sent(halo1.all + halo2.all)


def body(frames, g1, b1, w1, g2, b2, w2, lw):
    hbm, vmem = pl.BlockSpec(memory_space=pltpu.HBM), pl.BlockSpec(memory_space=pltpu.VMEM)
    dma = pltpu.SemaphoreType.DMA
    params = jnp.concatenate([lw.T.astype(F32)] + [v.reshape(1, 256) for v in (g1, b1, g2, b2)], axis=0)
    return pl.pallas_call(
        kernel,
        out_shape=[
            jax.ShapeDtypeStruct((4, 4, 128, 256), BF16),
            jax.ShapeDtypeStruct((4, 32, 256), BF16),
        ],
        in_specs=[hbm, vmem, hbm, hbm],
        out_specs=[hbm, vmem],
        scratch_shapes=[
            pltpu.VMEM((4, 4, 128, 256), BF16),
            pltpu.VMEM((4, 4, 128, 256), BF16),
            pltpu.VMEM((6, 6, 128, 256), BF16),
            pltpu.VMEM((6, 6, 128, 256), BF16),
            pltpu.VMEM((36, 160, 256), BF16),
            pltpu.VMEM((24, 160, 256), BF16),
            pltpu.VMEM((2, 512, 256), F32),
            pltpu.VMEM((3, 3, 3, 256, 256), BF16),
            pltpu.VMEM((3, 3, 3, 256, 256), BF16),
            pltpu.VMEM((2, 3, 3, 256, 256), BF16),
            pltpu.VMEM((2, 3, 3, 256, 256), BF16),
            pltpu.VMEM((128, 256), F32),
            pltpu.VMEM((128, 128), BF16),
            pltpu.VMEM((128, 128), BF16),
            pltpu.VMEM((256, 256), BF16),
            pltpu.VMEM((256, 256), BF16),
            pltpu.VMEM((16, 8, 256), F32),
            pltpu.VMEM((16, 8, 256), F32),
            pltpu.VMEM((8, 512), F32),
            pltpu.VMEM((16, 512), F32),
            pltpu.VMEM((8, 512), F32),
            pltpu.VMEM((16, 512), F32),
            dma((11,)),
            dma((4,)),
        ]
        + [dma((11,))] * 4
        + [dma((7,)), dma((7,)), dma((15,)), dma((15,))] * 2
        + [dma((16,)), dma((16,))],
        compiler_params=pltpu.CompilerParams(
            collective_id=0, has_side_effects=True, vmem_limit_bytes=54000 * 2**10
        ),
    )(frames, params, w1, w2)


def solution(mesh):
    return jax.shard_map(
        body,
        mesh=mesh,
        in_specs=(P("tm", "tile", None, None), P(), P(), P(), P(), P(), P(), P()),
        out_specs=(P("tm", "tile", None, None), P("tm", None, "tile")),
        check_vma=False,
    )
```

profile of v0, /device:TPU:1, one launch (start us, length us, event | category | flops | bytes accessed | tf_op | source)
XLA Modules:
  0.0 63.9 jit_solution(6820696082450023728)
XLA Ops:
  0.6 0.7 %convert_bitcast_fusion = f32[16,256]{1,0:T(8,128)S(1)} fusion(bf16[256,16]{0,1:T(8,128)(2,1)} %param.15), kind=kLoop, calls=%fused_computation | loop fusion | flops 4096 | bytes 24576 | tf_op jit(solution)/shard_map/convert_element_type | solution.py:415
  1.3 0.7 %concatenate.3.params = f32[20,256]{1,0:T(8,128)S(1)} concatenate(f32[16,256]{1,0:T(8,128)S(1)} %convert_bitcast_fusion, f32[1,256]{1,0:T(1,128)} %bitcast.6, f32[1,256]{1,0:T(1,128)} %bitcast.7, f32[1,256]{1,0:T(1,128)} %bitcast.8, f32[1,256]{1,0:T(1,128)} %bitcast.9), dimensions={0} | concatenate | bytes 40960 | tf_op jit(solution)/shard_map/concatenate | solution.py:415
  2.1 60.2 %shard_map.95 = (bf16[4,4,128,256]{3,2,1,0:T(8,128)(2,1)S(1)}, bf16[4,32,256]{2,1,0:T(8,128)(2,1)S(1)}) custom-call(bf16[4,4,128,256]{3,2,1,0:T(8,128)(2,1)} %x.1, f32[20,256]{1,0:T(8,128)S(1)} %concatenate.3.params, bf16[3,3,3,256,256]{4,3,2,1,0:T(8,128)(2,1)} %w1.1, bf16[3,3,3,256,256]{4,3,2,1,0:T(8,128)(2,1)} %w2.1), custom_call_target="tpu_custom_call" | custom-call | tf_op jit(solution)/shard_map/pallas_call | solution.py:416
  62.3 1.0 %copy.12 = bf16[4,4,128,256]{3,2,1,0:T(8,128)(2,1)} copy(bf16[4,4,128,256]{3,2,1,0:T(8,128)(2,1)S(1)} %get-tuple-element.4) | data formatting | bytes 2097152
  63.2 0.6 copy.13
where the time goes:
time: 64 us; the launch traced here: 63.9 us
  Pallas kernels  60.2 us (94%)
  local copies, waits for them, and re-layouts  2.35 us (4%)
  other arithmetic  0.7 us (1%)
  between operations  0.64 us (1%)
    pallas_call x1, Pallas kernels, body(): pl.pallas_call(kernel, out_shape=[jax.ShapeDtypeStruct((4, 4, 128, 256),...  60.2 us
    unnamed x2, local copies, waits for them, and re-layouts  1.6 us

commit v1 on v0

--- a/solution.py
+++ b/solution.py
@@ -24,7 +24,7 @@
 def kernel(
     x, params, w1, w2, feat, tok,
     raw, final, first, second, act, mixed, acc, taps1, taps2, blend1, blend2, rows, spread, back, latent, groups, outbox, inbox,
-    part1, part2, part3, part4, load_sem, out_sem, hs1, hr1, hs2, hr2, as1, ar1, as2, ar2, as3, ar3, as4, ar4, ts, tr,
+    part1, part2, part3, part4, load_sem, hs1, hr1, hs2, hr2, as1, ar1, as2, ar2, as3, ar3, as4, ar4, ts, tr,
 ):
     tm, tile = lax.axis_index("tm"), lax.axis_index("tile")
     times, tiles = 8, 16
@@ -370,8 +370,7 @@
 
     def finish_features(o):
         for r in range(4):
-            raw[o, r] = mm(back[...], final[o, r]).astype(BF16)
-        pltpu.make_async_copy(raw.at[o], feat.at[o], out_sem.at[o]).start()
+            feat[o, r] = mm(back[...], final[o, r]).astype(BF16)
 
     def finish(o, half, carry):
         finish_latents(o + half, half)
@@ -400,8 +399,6 @@
         source = lax.rem(tile + tiles - k, tiles)
         send(outbox.at[source], inbox.at[source], ts.at[k], tr.at[k], dev(tm, source)).wait_recv()
     tok[...] = mm(turn, inbox[...].reshape(128, 256).astype(BF16)).astype(BF16).reshape(4, 32, 256)
-    for f in range(4):
-        pltpu.make_async_copy(raw.at[f], feat.at[f], out_sem.at[f]).wait()
     for copy in copies:
         copy.wait_send()
     totals1.sent()
@@ -420,7 +417,7 @@
             jax.ShapeDtypeStruct((4, 32, 256), BF16),
         ],
         in_specs=[hbm, vmem, hbm, hbm],
-        out_specs=[hbm, vmem],
+        out_specs=[vmem, vmem],
         scratch_shapes=[
             pltpu.VMEM((4, 4, 128, 256), BF16),
             pltpu.VMEM((4, 4, 128, 256), BF16),
@@ -445,7 +442,6 @@
             pltpu.VMEM((8, 512), F32),
             pltpu.VMEM((16, 512), F32),
             dma((11,)),
-            dma((4,)),
         ]
         + [dma((11,))] * 4
         + [dma((7,)), dma((7,)), dma((15,)), dma((15,))] * 2

time: 64 us -> 63.8 us (level)
  no operation moved by 1% of the time
where the time goes in v1:
time: 63.8 us; the launch traced here: 63.5 us
  Pallas kernels  59.8 us (94%)
  local copies, waits for them, and re-layouts  2.35 us (4%)
  other arithmetic  0.7 us (1%)
  between operations  0.64 us (1%)
    pallas_call x1, Pallas kernels, body(): pl.pallas_call(kernel, out_shape=[jax.ShapeDtypeStruct((4, 4, 128, 256),...  59.8 us
    unnamed x2, local copies, waits for them, and re-layouts  1.6 us

profile of v1, /device:TPU:1, one launch (start us, length us, event | category | flops | bytes accessed | tf_op | source)
XLA Modules:
  0.0 63.5 jit_solution(6695343547893170813)
XLA Ops:
  0.6 0.7 %convert_bitcast_fusion = f32[16,256]{1,0:T(8,128)S(1)} fusion(bf16[256,16]{0,1:T(8,128)(2,1)} %param.15), kind=kLoop, calls=%fused_computation | loop fusion | flops 4096 | bytes 24576 | tf_op jit(solution)/shard_map/convert_element_type | solution.py:412
  1.3 0.7 %concatenate.3.params = f32[20,256]{1,0:T(8,128)S(1)} concatenate(f32[16,256]{1,0:T(8,128)S(1)} %convert_bitcast_fusion, f32[1,256]{1,0:T(1,128)} %bitcast.6, f32[1,256]{1,0:T(1,128)} %bitcast.7, f32[1,256]{1,0:T(1,128)} %bitcast.8, f32[1,256]{1,0:T(1,128)} %bitcast.9), dimensions={0} | concatenate | bytes 40960 | tf_op jit(solution)/shard_map/concatenate | solution.py:412
  2.1 59.8 %shard_map.95 = (bf16[4,4,128,256]{3,2,1,0:T(8,128)(2,1)S(1)}, bf16[4,32,256]{2,1,0:T(8,128)(2,1)S(1)}) custom-call(bf16[4,4,128,256]{3,2,1,0:T(8,128)(2,1)} %x.1, f32[20,256]{1,0:T(8,128)S(1)} %concatenate.3.params, bf16[3,3,3,256,256]{4,3,2,1,0:T(8,128)(2,1)} %w1.1, bf16[3,3,3,256,256]{4,3,2,1,0:T(8,128)(2,1)} %w2.1), custom_call_target="tpu_custom_call" | custom-call | tf_op jit(solution)/shard_map/pallas_call | solution.py:413
  61.9 1.0 %copy.12 = bf16[4,4,128,256]{3,2,1,0:T(8,128)(2,1)} copy(bf16[4,4,128,256]{3,2,1,0:T(8,128)(2,1)S(1)} %get-tuple-element.4) | data formatting | bytes 2097152
  62.8 0.6 copy.13
